TPU v7x, 32 devices: a whole 2x2x4 slice. The times are simulated.
32 devices in a mesh: seq: 8 (over y, x, core), tp: 4 (over z).
Axes of the slice: x: 2, y: 2, z: 4, core: 2. Of those that a mesh axis runs over, the one named last changes fastest.
Arguments:
- query_heads: bfloat16 [4096, 2048], P('seq', 'tp'), may hold values from -120 to 120
- key_heads: bfloat16 [4096, 2048], P('seq', 'tp'), may hold values from -120 to 120
- value_heads: bfloat16 [4096, 2048], P('seq', 'tp'), may hold values from -6 to 6
- out_weight: bfloat16 [2048, 2048], P('tp'), may hold values from -0.125 to 0.125
- cotangent: bfloat16 [4096, 2048], P('seq', 'tp'), may hold values from -6 to 6
- loss_mask: int32 [4096], P('seq'), may hold values 0 or 1
- block_pattern: int32 [16, 9], replicated, may hold values from 0 to 15, as said below
- block_counts: int32 [16], replicated, may hold values from 1 to 9
Outputs:
- attended: bfloat16 [4096, 2048], P('seq', 'tp')
- query_grad: bfloat16 [4096, 2048], P('seq', 'tp')
- key_grad: bfloat16 [4096, 2048], P('seq', 'tp')
- value_grad: bfloat16 [4096, 2048], P('seq', 'tp')
- weight_grad: float32 [2048, 2048], P('tp', 'seq')
Inputs may be any that keep to these rules, and one draw needn't show every extreme that they name: For j < block_counts[b], block_pattern[b, j] are distinct blocks within 4 of b, the first being b itself; later entries are ignored.
All inputs are finite; a program needn't handle non-finite values. No bound on the sum of `loss_mask` on one device may be relied on, other than what follows from the above.
Results may differ from a plain program's by a relative error of at most 0.035.
Values may be sent and summed in bfloat16 or wider, within the bound.
A program may use at most 192 MiB of HBM per device.

v0:
```python
import math

import jax
import jax.numpy as jnp
from jax import lax
from jax.sharding import PartitionSpec as P

HD = 128
BLK = 256
WINDOW = 4


FLOOR_LOGIT = -1e30


def passed_along(value, axis, steps):
    count = lax.axis_size(axis)
    leading, last = (max(0, -steps), min(count, count - steps))
    return lax.ppermute(value, axis, [(source, source + steps) for source in range(leading, last)])


def listed_table(block_pattern, block_counts, query_first, query_count, key_first, key_count):
    query_lists = lax.dynamic_slice_in_dim(block_pattern, query_first, query_count, 0)
    list_sizes = lax.dynamic_slice_in_dim(block_counts, query_first, query_count, 0)
    slot_ids = jnp.arange(block_pattern.shape[1], dtype=jnp.int32)
    in_use = slot_ids[None, :] < list_sizes[:, None]
    key_ids = key_first + jnp.arange(key_count, dtype=jnp.int32)
    matched = (query_lists[:, :, None] == key_ids[None, None, :]) & in_use[:, :, None]
    return jnp.any(matched, axis=1)


def masked_logits(query_part, key_part, listed):
    logits = jnp.einsum(
        "qhd,khd->hqk", query_part, key_part, preferred_element_type=jnp.float32
    ) * (1.0 / math.sqrt(HD))
    head_count, query_len, key_len = logits.shape
    blocked = logits.reshape(
        head_count,
        listed.shape[0],
        query_len // listed.shape[0],
        listed.shape[1],
        key_len // listed.shape[1],
    )
    blocked = jnp.where(listed[None, :, None, :, None], blocked, FLOOR_LOGIT)
    return blocked.reshape(head_count, query_len, key_len)


def piece_logits(query_part, key_part, listed):

    def compute(unused):
        return masked_logits(query_part, key_part, listed)

    def skipped(unused):
        return jnp.full(
            (query_part.shape[1], query_part.shape[0], key_part.shape[0]), FLOOR_LOGIT, jnp.float32
        )

    return lax.cond(jnp.any(listed), compute, skipped, 0)


def piece_output(logits, log_total, value_part, listed):

    def compute(unused):
        weights_b = jnp.exp(logits - log_total[:, :, None]).astype(jnp.bfloat16)
        return jnp.einsum("hqk,khd->hqd", weights_b, value_part, preferred_element_type=jnp.float32)

    def skipped(unused):
        return jnp.zeros((logits.shape[0], logits.shape[1], value_part.shape[2]), jnp.float32)

    return lax.cond(jnp.any(listed), compute, skipped, 0)


def pair_terms(
    logits,
    query_part,
    grad_part,
    log_total,
    row_dots,
    key_part,
    value_part,
    listed,
    want_query,
    want_keys,
):
    query_shape = query_part.shape
    key_shape = key_part.shape

    def compute(unused):
        scores = masked_logits(query_part, key_part, listed) if logits is None else logits
        weights = jnp.exp(scores - log_total[:, :, None])
        d_probs = jnp.einsum(
            "qhd,khd->hqk", grad_part, value_part, preferred_element_type=jnp.float32
        )
        d_logits = (weights * (d_probs - row_dots[:, :, None]) * (1.0 / math.sqrt(HD))).astype(
            jnp.bfloat16
        )
        query_term = jnp.zeros(query_shape, jnp.float32)
        key_term = jnp.zeros(key_shape, jnp.float32)
        value_term = jnp.zeros(key_shape, jnp.float32)
        if want_query:
            query_term = jnp.einsum(
                "hqk,khd->qhd", d_logits, key_part, preferred_element_type=jnp.float32
            )
        if want_keys:
            key_term = jnp.einsum(
                "hqk,qhd->khd", d_logits, query_part, preferred_element_type=jnp.float32
            )
            value_term = jnp.einsum(
                "hqk,qhd->khd",
                weights.astype(jnp.bfloat16),
                grad_part,
                preferred_element_type=jnp.float32,
            )
        return (query_term, key_term, value_term)

    def skipped(unused):
        return (
            jnp.zeros(query_shape, jnp.float32),
            jnp.zeros(key_shape, jnp.float32),
            jnp.zeros(key_shape, jnp.float32),
        )

    return lax.cond(jnp.any(listed), compute, skipped, 0)


def local(
    query_heads,
    key_heads,
    value_heads,
    out_weight,
    cotangent,
    loss_mask,
    block_pattern,
    block_counts,
):
    tok_rows = query_heads.shape[0]
    local_cols = query_heads.shape[1]
    head_count = local_cols // HD
    query_blocks = tok_rows // BLK
    seq_devices = lax.axis_size("seq")
    reach_dev = min((WINDOW * BLK + tok_rows - 1) // tok_rows, seq_devices - 1)
    position = lax.axis_index("seq")
    own_first = position * query_blocks
    query_part = query_heads.reshape(tok_rows, head_count, HD)
    offsets = [distance for distance in range(-reach_dev, reach_dev + 1) if distance != 0]
    neighbours = []
    for distance in offsets:
        arrived = passed_along((key_heads, value_heads), "seq", distance)
        neighbours.append((position - distance, arrived[0], arrived[1]))
    pieces = [(position, key_heads, value_heads)] + neighbours
    prepared = []
    for source, key_piece, value_piece in pieces:
        listed = listed_table(
            block_pattern,
            block_counts,
            own_first,
            query_blocks,
            source * query_blocks,
            query_blocks,
        )
        key_part = key_piece.reshape(tok_rows, head_count, HD)
        value_part = value_piece.reshape(tok_rows, head_count, HD)
        prepared.append((listed, key_part, value_part, piece_logits(query_part, key_part, listed)))
    highest = jnp.full((head_count, tok_rows), FLOOR_LOGIT, jnp.float32)
    for listed, key_part, value_part, logits in prepared:
        highest = jnp.maximum(highest, jnp.max(logits, axis=2))
    denominator = jnp.zeros((head_count, tok_rows), jnp.float32)
    for listed, key_part, value_part, logits in prepared:
        denominator = denominator + jnp.sum(jnp.exp(logits - highest[:, :, None]), axis=2)
    log_total = highest + jnp.log(denominator)
    weighted = jnp.zeros((head_count, tok_rows, HD), jnp.float32)
    for listed, key_part, value_part, logits in prepared:
        weighted = weighted + piece_output(logits, log_total, value_part, listed)
    heads_out = (
        jnp.transpose(weighted, (1, 0, 2)).reshape(tok_rows, local_cols).astype(jnp.bfloat16)
    )
    partial_out = jnp.dot(heads_out, out_weight, preferred_element_type=jnp.float32)
    attended = lax.psum_scatter(partial_out, "tp", scatter_dimension=1, tiled=True).astype(
        jnp.bfloat16
    )
    masked = jnp.where(loss_mask[:, None] == 1, cotangent, jnp.zeros_like(cotangent))
    full_grad = lax.all_gather(masked, "tp", axis=1, tiled=True)
    weight_part = jnp.einsum("tc,td->cd", heads_out, full_grad, preferred_element_type=jnp.float32)
    weight_grad = lax.psum_scatter(weight_part, "seq", scatter_dimension=1, tiled=True)
    d_heads = jnp.einsum(
        "td,cd->tc", full_grad, out_weight, preferred_element_type=jnp.float32
    ).astype(jnp.bfloat16)
    grad_part = d_heads.reshape(tok_rows, head_count, HD)
    row_dots = jnp.sum(
        grad_part.astype(jnp.float32)
        * heads_out.reshape(tok_rows, head_count, HD).astype(jnp.float32),
        axis=2,
    ).T
    own_listed, own_keys, own_values, own_logits = prepared[0]
    term_set = pair_terms(
        own_logits,
        query_part,
        grad_part,
        log_total,
        row_dots,
        own_keys,
        own_values,
        own_listed,
        True,
        True,
    )
    query_acc, key_acc, value_acc = term_set
    for listed, key_part, value_part, logits in prepared[1:]:
        term_set = pair_terms(
            logits,
            query_part,
            grad_part,
            log_total,
            row_dots,
            key_part,
            value_part,
            listed,
            True,
            False,
        )
        query_acc = query_acc + term_set[0]
    for distance in offsets:
        arrived = passed_along((query_heads, d_heads), "seq", distance)
        arrived_stats = passed_along((log_total, row_dots), "seq", distance)
        sender = position - distance
        inside = (sender >= 0) & (sender < seq_devices)
        listed = (
            listed_table(
                block_pattern,
                block_counts,
                sender * query_blocks,
                query_blocks,
                own_first,
                query_blocks,
            )
            & inside
        )
        term_set = pair_terms(
            None,
            arrived[0].reshape(tok_rows, head_count, HD),
            arrived[1].reshape(tok_rows, head_count, HD),
            arrived_stats[0],
            arrived_stats[1],
            own_keys,
            own_values,
            listed,
            False,
            True,
        )
        key_acc = key_acc + term_set[1]
        value_acc = value_acc + term_set[2]
    query_grad = query_acc.reshape(tok_rows, local_cols).astype(jnp.bfloat16)
    key_grad = key_acc.reshape(tok_rows, local_cols).astype(jnp.bfloat16)
    value_grad = value_acc.reshape(tok_rows, local_cols).astype(jnp.bfloat16)
    return (attended, query_grad, key_grad, value_grad, weight_grad)


def solution(mesh):
    in_specs = (
        P("seq", "tp"),
        P("seq", "tp"),
        P("seq", "tp"),
        P("tp", None),
        P("seq", "tp"),
        P("seq"),
        P(),
        P(),
    )
    out_specs = (P("seq", "tp"), P("seq", "tp"), P("seq", "tp"), P("seq", "tp"), P("tp", "seq"))
    return jax.shard_map(local, mesh=mesh, in_specs=in_specs, out_specs=out_specs, check_vma=False)
```

profile of v0, /device:TPU:2, one launch (start us, length us, event | category | flops | bytes accessed | tf_op | source)
XLA Modules:
  0.0 337.9 jit_solution(5042369883760982509)
XLA Ops:
  37.2 6.8 %conditional.19 = (f32[4,512,512]{1,2,0:T(8,128)}, f32[4,512]{1,0:T(4,128)}, f32[4,512,1]{1,0,2:T(4,128)S(1)}) conditional(s32[]{:T(128)} %convert_element_type.136, () %tuple.153, (pred[2,9,2]{1,2,0:T(4,128)(4,1)S(1)}, bf16[512,4,128]{0,2,1:T(8,128)(2,1)S(1)}, bf16[512,4,128]{0,2,1:T(8,128)(2,1)S(1)}) %tuple.336), branch_computations={%region_1.0_spmd, %region_2.5_spmd} | conditional | flops 271579168 | bytes 6840389 | solution.py:58
  51.5 7.0 %conditional.20 = (f32[4,512,512]{1,2,0:T(8,128)}, f32[4,512]{1,0:T(4,128)}, f32[4,512,1]{1,0,2:T(4,128)S(1)}) conditional(s32[]{:T(128)} %convert_element_type.137, () %tuple.155, (pred[2,9,2]{1,2,0:T(4,128)(4,1)S(1)}, bf16[512,4,128]{0,2,1:T(8,128)(2,1)S(1)}, bf16[512,4,128]{0,2,1:T(8,128)(2,1)}) %tuple.337), branch_computations={%region_6.7_spmd, %region_7.10_spmd} | conditional | flops 271579168 | bytes 6840389 | solution.py:58
  58.6 7.0 %conditional.23 = (f32[4,512,512]{1,2,0:T(8,128)}, f32[4,512]{1,0:T(4,128)}, f32[4,512,1]{1,0,2:T(4,128)S(1)}) conditional(s32[]{:T(128)} %convert_element_type.140, () %tuple.161, (pred[2,9,2]{1,2,0:T(4,128)(4,1)S(1)}, bf16[512,4,128]{0,2,1:T(8,128)(2,1)S(1)}, bf16[512,4,128]{0,2,1:T(8,128)(2,1)}) %tuple.338), branch_computations={%region_21.22_spmd, %region_22.25_spmd} | conditional | flops 271579168 | bytes 6840389 | solution.py:58
  65.6 6.9 %conditional.22 = (f32[4,512,512]{1,2,0:T(8,128)}, f32[4,512]{1,0:T(4,128)}, f32[4,512,1]{1,0,2:T(4,128)S(1)}) conditional(s32[]{:T(128)} %convert_element_type.139, () %tuple.159, (pred[2,9,2]{1,2,0:T(4,128)(4,1)S(1)}, bf16[512,4,128]{0,2,1:T(8,128)(2,1)S(1)}, bf16[512,4,128]{0,2,1:T(8,128)(2,1)}) %tuple.339), branch_computations={%region_16.17_spmd, %region_17.20_spmd} | conditional | flops 271579168 | bytes 6840389 | solution.py:58
  72.5 7.2 %conditional.21 = (f32[4,512,512]{1,2,0:T(8,128)}, f32[4,512]{1,0:T(4,128)}, f32[4,512,1]{1,0,2:T(4,128)S(1)}) conditional(s32[]{:T(128)} %convert_element_type.138, () %tuple.157, (pred[2,9,2]{1,2,0:T(4,128)(4,1)S(1)}, bf16[512,4,128]{0,2,1:T(8,128)(2,1)S(1)}, bf16[512,4,128]{0,2,1:T(8,128)(2,1)}) %tuple.340), branch_computations={%region_11.12_spmd, %region_12.15_spmd} | conditional | flops 271579168 | bytes 6840389 | solution.py:58
  79.7 8.5 %exponential_reduce_fusion.3 = (f32[4,512]{1,0:T(4,128)S(1)}, f32[4,512]{1,0:T(4,128)S(1)}, f32[4,512]{1,0:T(4,128)S(1)}, f32[4,512]{1,0:T(4,128)S(1)}, f32[4,512]{1,0:T(4,128)S(1)}) fusion(f32[4,512,512]{1,2,0:T(8,128)} %get-tuple-element.369, f32[4,512]{1,0:T(4,128)S(1)} %maximum_bitcast_fusion, f32[4,512,512]{1,2,0:T(8,128)} %get-tuple-element.370, ...), kind=kLoop, calls=%fused_computation.141 | loop fusion | flops 10475520 | bytes 21020672 | tf_op jit(solution)/shard_map/reduce_sum | solution.py:169
  96.9 9.5 %conditional.28 = (f32[4,512,128]{1,2,0:T(8,128)}) conditional(s32[]{:T(128)} %convert_element_type.140, () %tuple.170, (f32[4,512]{1,0:T(4,128)S(1)}, f32[4,512,512]{1,2,0:T(8,128)}, bf16[512,4,128]{2,1,0:T(4,128)(2,1)}) %tuple.171), branch_computations={%region_38.39_spmd, %region_39.40_spmd} | conditional | flops 270532608 | bytes 14163976 | solution.py:70
  106.4 9.6 %conditional.27 = (f32[4,512,128]{1,2,0:T(8,128)}) conditional(s32[]{:T(128)} %convert_element_type.139, () %tuple.168, (f32[4,512]{1,0:T(4,128)S(1)}, f32[4,512,512]{1,2,0:T(8,128)}, bf16[512,4,128]{2,1,0:T(4,128)(2,1)}) %tuple.169), branch_computations={%region_36.37_spmd, %region_37.38_spmd} | conditional | flops 270532608 | bytes 14163976 | solution.py:70
  116.0 9.5 %conditional.26 = (f32[4,512,128]{1,2,0:T(8,128)}) conditional(s32[]{:T(128)} %convert_element_type.138, () %tuple.166, (f32[4,512]{1,0:T(4,128)S(1)}, f32[4,512,512]{1,2,0:T(8,128)}, bf16[512,4,128]{2,1,0:T(4,128)(2,1)}) %tuple.167), branch_computations={%region_34.35_spmd, %region_35.36_spmd} | conditional | flops 270532608 | bytes 14163976 | solution.py:70
  125.5 9.5 %conditional.24 = (f32[4,512,128]{1,2,0:T(8,128)}) conditional(s32[]{:T(128)} %convert_element_type.136, () %tuple.152, (f32[4,512]{1,0:T(4,128)S(1)}, f32[4,512,512]{1,2,0:T(8,128)}, bf16[512,4,128]{2,1,0:T(4,128)(2,1)}) %tuple.163), branch_computations={%region_30.31_spmd, %region_31.32_spmd} | conditional | flops 270532608 | bytes 14163976 | solution.py:70
  135.0 9.9 %conditional.25 = (f32[4,512,128]{1,2,0:T(8,128)}) conditional(s32[]{:T(128)} %convert_element_type.137, () %tuple.164, (f32[4,512]{1,0:T(4,128)S(1)}, f32[4,512,512]{1,2,0:T(8,128)}, bf16[512,4,128]{2,1,0:T(4,128)(2,1)}) %tuple.165), branch_computations={%region_32.33_spmd, %region_33.34_spmd} | conditional | flops 270532608 | bytes 14163976 | solution.py:70
  181.4 9.3 %collective-permute-start.22 = (bf16[512,512]{0,1:T(8,128)(2,1)}, bf16[512,512]{0,1:T(8,128)(2,1)}, u32[]{:S(2)}, u32[]{:S(2)}) collective-permute-start(bf16[512,512]{0,1:T(8,128)(2,1)} %convolution_convert_fusion), channel_id=1, source_target_pairs={{0,8},{4,12},{8,16},{12,20},{16,24},{20,28},{1,9},{5,13},{9,17},{1... | collective-permute-start | bytes 1572872 | tf_op jit(solution)/shard_map/ppermute | solution.py:19
  210.6 9.5 %conditional.33 = (f32[512,4,128]{2,0,1:T(8,128)S(1)}) conditional(s32[]{:T(128)} %convert_element_type.140, () %tuple.180, (f32[4,512]{1,0:T(4,128)S(1)}, f32[4,512,512]{1,2,0:T(8,128)}, bf16[512,4,128]{0,2,1:T(8,128)(2,1)}, bf16[512,4,128]{2,1,0:T(4,128)(2,1)S(1)}, f32[4,512]{1,0:T(4,128)S(1)}, /*index=5*/bf16[512,4,128]{0,2,1:T(8,128)(2,1)}) %tuple.350), branch_computations={%region_50.51_spmd, %region_51.52_spmd} | conditional | flops 542113792 | bytes 15220744 | solution.py:123
  221.2 9.6 %conditional.32 = (f32[512,4,128]{2,0,1:T(8,128)S(1)}) conditional(s32[]{:T(128)} %convert_element_type.139, () %tuple.178, (f32[4,512]{1,0:T(4,128)S(1)}, f32[4,512,512]{1,2,0:T(8,128)}, bf16[512,4,128]{0,2,1:T(8,128)(2,1)}, bf16[512,4,128]{2,1,0:T(4,128)(2,1)}, f32[4,512]{1,0:T(4,128)S(1)}, /*index=5*/bf16[512,4,128]{0,2,1:T(8,128)(2,1)}) %tuple.351), branch_computations={%region_48.49_spmd, %region_49.50_spmd} | conditional | flops 542113792 | bytes 15220744 | solution.py:123
  231.7 9.6 %conditional.31 = (f32[512,4,128]{2,0,1:T(8,128)S(1)}) conditional(s32[]{:T(128)} %convert_element_type.138, () %tuple.176, (f32[4,512]{1,0:T(4,128)S(1)}, f32[4,512,512]{1,2,0:T(8,128)}, bf16[512,4,128]{0,2,1:T(8,128)(2,1)}, bf16[512,4,128]{2,1,0:T(4,128)(2,1)}, f32[4,512]{1,0:T(4,128)S(1)}, /*index=5*/bf16[512,4,128]{0,2,1:T(8,128)(2,1)}) %tuple.352), branch_computations={%region_46.47_spmd, %region_47.48_spmd} | conditional | flops 542113792 | bytes 15220744 | solution.py:123
  242.3 15.8 %conditional.29 = (f32[512,4,128]{2,0,1:T(8,128)S(1)}, f32[512,4,128]{2,0,1:T(8,128)}, f32[512,4,128]{2,0,1:T(8,128)S(1)}) conditional(s32[]{:T(128)} %convert_element_type.136, () %tuple.172, (f32[4,512]{1,0:T(4,128)S(1)}, f32[4,512,512]{1,2,0:T(8,128)}, bf16[512,4,128]{0,2,1:T(8,128)(2,1)}, bf16[512,4,128]{2,1,0:T(4,128)(2,1)}, ...), branch_computations={%region_42.43_spmd, %region_43.44_spmd} | conditional | flops 1081081856 | bytes 49832016 | solution.py:123
  242.4 5.3 %copy.122 = f32[4,512,512]{2,1,0:T(8,128)} copy(f32[4,512,512]{1,2,0:T(8,128)} %get-tuple-element.489) | data formatting | bytes 8388608 | tf_op jit(solution)/shard_map
  259.1 10.8 %conditional.30 = (f32[512,4,128]{2,0,1:T(8,128)}) conditional(s32[]{:T(128)} %convert_element_type.137, () %tuple.174, (f32[4,512]{1,0:T(4,128)S(1)}, f32[4,512,512]{1,2,0:T(8,128)}, bf16[512,4,128]{0,2,1:T(8,128)(2,1)}, bf16[512,4,128]{2,1,0:T(4,128)(2,1)}, f32[4,512]{1,0:T(4,128)S(1)}, /*index=5*/bf16[512,4,128]{0,2,1:T(8,128)(2,1)}) %tuple.354), branch_computations={%region_44.45_spmd, %region_45.46_spmd} | conditional | flops 542113792 | bytes 17317924 | solution.py:123
  259.1 5.7 %copy.127 = f32[4,512,512]{2,1,0:T(8,128)} copy(f32[4,512,512]{1,2,0:T(8,128)} %get-tuple-element.496) | data formatting | bytes 8388608 | tf_op jit(solution)/shard_map
  277.2 12.3 %conditional.37 = (f32[512,4,128]{2,0,1:T(8,128)S(1)}, f32[512,4,128]{2,0,1:T(8,128)S(1)}) conditional(s32[]{:T(128)} %convert_element_type.153, () %tuple.188, (pred[2,2]{1,0:T(4,128)(4,1)S(1)}, bf16[512,512]{1,0:T(8,128)(2,1)S(1)}, bf16[512,4,128]{0,2,1:T(8,128)(2,1)S(1)}, f32[4,512]{1,0:T(4,128)S(1)}, bf16[512,512]{0,1:T(8,128)(2,1)}, ...), branch_computations={%region_66.67_spmd, %region_67.68_spmd} | conditional | flops 1085276160 | bytes 21258288 | solution.py:123
  290.8 15.1 %conditional.36 = (f32[512,4,128]{2,0,1:T(8,128)}, f32[512,4,128]{2,0,1:T(8,128)}) conditional(s32[]{:T(128)} %convert_element_type.152, () %tuple.186, (pred[2,2]{1,0:T(4,128)(4,1)S(1)}, bf16[512,512]{1,0:T(8,128)(2,1)}, bf16[512,4,128]{0,2,1:T(8,128)(2,1)S(1)}, f32[4,512]{1,0:T(4,128)S(1)}, bf16[512,512]{0,1:T(8,128)(2,1)}, ...), branch_computations={%region_62.63_spmd, %region_63.64_spmd} | conditional | flops 1085276160 | bytes 19161108 | solution.py:123
  295.2 5.9 %fusion.97 = f32[512,4,128]{2,0,1:T(8,128)} fusion(f32[4,512,512]{2,1,0:T(8,128)} %fusion.102, bf16[512,4,128]{0,2,1:T(8,128)(2,1)} %bitcast.18, f32[4,512]{1,0:T(4,128)S(1)} %get-tuple-element.319, f32[4,512]{1,0:T(4,128)S(1)} %get-tuple-element.316, pred[512,512]{1,0:T(8,128)(4,1)S(1)} %bitcast.216, bf16[512,4,128]{2,1,0:T(4,128)(2,1)S(1)} %get-tuple-element.318, ...), kind=kOutput, calls=%fused_computation.105 | convolution fusion | flops 544210944 | bytes 7094272 | tf_op jit(solution)/shard_map/cond/branch_1_fun/hqk,qhd->khd/dot_general | solution.py:105
  307.4 15.1 %conditional.34 = (f32[512,4,128]{2,0,1:T(8,128)}, f32[512,4,128]{2,0,1:T(8,128)}) conditional(s32[]{:T(128)} %convert_element_type.150, () %tuple.182, (pred[2,2]{1,0:T(4,128)(4,1)S(1)}, bf16[512,512]{1,0:T(8,128)(2,1)}, bf16[512,4,128]{0,2,1:T(8,128)(2,1)S(1)}, f32[4,512]{1,0:T(4,128)S(1)}, bf16[512,512]{0,1:T(8,128)(2,1)}, ...), branch_computations={%region_54.55_spmd, %region_55.56_spmd} | conditional | flops 1085276160 | bytes 19161108 | solution.py:123
  311.8 5.9 %fusion.51 = f32[512,4,128]{2,0,1:T(8,128)} fusion(f32[4,512,512]{2,1,0:T(8,128)} %fusion.56, bf16[512,4,128]{0,2,1:T(8,128)(2,1)} %bitcast.12, f32[4,512]{1,0:T(4,128)S(1)} %get-tuple-element.305, f32[4,512]{1,0:T(4,128)S(1)} %get-tuple-element.302, pred[512,512]{1,0:T(8,128)(4,1)S(1)} %bitcast.220, bf16[512,4,128]{2,1,0:T(4,128)(2,1)S(1)} %get-tuple-element.304, ...), kind=kOutput, calls=%fused_computation.63 | convolution fusion | flops 544210944 | bytes 7094272 | tf_op jit(solution)/shard_map/cond/branch_1_fun/hqk,qhd->khd/dot_general | solution.py:105
  (205 shorter events, 275.5 us)
Async XLA Ops:
  7.2 137.8 %all-gather.2.cloned.1.call-start = ((), (), s32[]{:S(2)}) async-start(), calls=%async_computation.3 | async-start | bytes 2621440 | tf_op jit(solution)/shard_map/all_gather | solution.py:182
  10.1 318.8 %reduce-scatter.3.cloned.1.call-start = ((), (), s32[]{:S(2)}) async-start(), calls=%async_computation.2 | async-start | bytes 5242880 | tf_op jit(solution)/shard_map/reduce_scatter | solution.py:178
  11.4 32.6 %collective-permute-start = (bf16[512,512]{0,1:T(8,128)(2,1)S(1)}, bf16[512,512]{0,1:T(8,128)(2,1)}, u32[]{:S(2)}, u32[]{:S(2)}) collective-permute-start(bf16[512,512]{0,1:T(8,128)(2,1)S(1)} %copy.92), channel_id=1, source_target_pairs={{8,0},{12,4},{16,8},{20,12},{24,16},{28,20},{9,1},{13,5},{17,9},{2... | collective-permute-start | bytes 1572872 | tf_op jit(solution)/shard_map/ppermute | solution.py:19
  13.3 32.6 %collective-permute-start.3 = (bf16[512,512]{0,1:T(8,128)(2,1)S(1)}, bf16[512,512]{0,1:T(8,128)(2,1)}, u32[]{:S(2)}, u32[]{:S(2)}) collective-permute-start(bf16[512,512]{0,1:T(8,128)(2,1)S(1)} %copy.92), channel_id=1, source_target_pairs={{0,8},{4,12},{8,16},{12,20},{16,24},{20,28},{1,9},{5,13},{9,17},{1... | collective-permute-start | bytes 1572872 | tf_op jit(solution)/shard_map/ppermute | solution.py:19
  18.1 31.5 %collective-permute-start.2 = (bf16[512,512]{0,1:T(8,128)(2,1)S(1)}, bf16[512,512]{0,1:T(8,128)(2,1)}, u32[]{:S(2)}, u32[]{:S(2)}) collective-permute-start(bf16[512,512]{0,1:T(8,128)(2,1)S(1)} %copy.92), channel_id=1, source_target_pairs={{0,4},{4,8},{8,12},{12,16},{16,20},{20,24},{24,28},{1,5},{5,9},{9,... | collective-permute-start | bytes 1572872 | tf_op jit(solution)/shard_map/ppermute | solution.py:19
  20.0 31.5 %collective-permute-start.1 = (bf16[512,512]{0,1:T(8,128)(2,1)S(1)}, bf16[512,512]{0,1:T(8,128)(2,1)}, u32[]{:S(2)}, u32[]{:S(2)}) collective-permute-start(bf16[512,512]{0,1:T(8,128)(2,1)S(1)} %copy.92), channel_id=1, source_target_pairs={{4,0},{8,4},{12,8},{16,12},{20,16},{24,20},{28,24},{5,1},{9,5},{13... | collective-permute-start | bytes 1572872 | tf_op jit(solution)/shard_map/ppermute | solution.py:19
  23.7 64.5 %collective-permute-start.7 = (bf16[512,512]{1,0:T(8,128)(2,1)}, bf16[512,512]{1,0:T(8,128)(2,1)}, u32[]{:S(2)}, u32[]{:S(2)}) collective-permute-start(bf16[512,512]{1,0:T(8,128)(2,1)} %param.48), channel_id=1, source_target_pairs={{0,8},{4,12},{8,16},{12,20},{16,24},{20,28},{1,9},{5,13},{9,17},{1... | collective-permute-start | bytes 1572872 | tf_op jit(solution)/shard_map/ppermute | solution.py:19
  44.0 47.0 %collective-permute-start.6 = (bf16[512,512]{1,0:T(8,128)(2,1)}, bf16[512,512]{1,0:T(8,128)(2,1)}, u32[]{:S(2)}, u32[]{:S(2)}) collective-permute-start(bf16[512,512]{1,0:T(8,128)(2,1)} %param.48), channel_id=1, source_target_pairs={{0,4},{4,8},{8,12},{12,16},{16,20},{20,24},{24,28},{1,5},{5,9},{9,... | collective-permute-start | bytes 1572872 | tf_op jit(solution)/shard_map/ppermute | solution.py:19
  45.9 47.0 %collective-permute-start.5 = (bf16[512,512]{1,0:T(8,128)(2,1)}, bf16[512,512]{1,0:T(8,128)(2,1)}, u32[]{:S(2)}, u32[]{:S(2)}) collective-permute-start(bf16[512,512]{1,0:T(8,128)(2,1)} %param.48), channel_id=1, source_target_pairs={{4,0},{8,4},{12,8},{16,12},{20,16},{24,20},{28,24},{5,1},{9,5},{13... | collective-permute-start | bytes 1572872 | tf_op jit(solution)/shard_map/ppermute | solution.py:19
  49.6 45.3 %collective-permute-start.4 = (bf16[512,512]{1,0:T(8,128)(2,1)}, bf16[512,512]{1,0:T(8,128)(2,1)}, u32[]{:S(2)}, u32[]{:S(2)}) collective-permute-start(bf16[512,512]{1,0:T(8,128)(2,1)} %param.48), channel_id=1, source_target_pairs={{8,0},{12,4},{16,8},{20,12},{24,16},{28,20},{9,1},{13,5},{17,9},{2... | collective-permute-start | bytes 1572872 | tf_op jit(solution)/shard_map/ppermute | solution.py:19
  156.0 174.9 %reduce-scatter.5.cloned.1.call-start = ((), (), s32[]{:S(2)}) async-start(), calls=%async_computation.4 | async-start | bytes 4718592 | tf_op jit(solution)/shard_map/reduce_scatter | solution.py:184
  161.9 17.5 %collective-permute-start.20 = (bf16[512,512]{1,0:T(8,128)(2,1)}, bf16[512,512]{1,0:T(8,128)(2,1)S(1)}, u32[]{:S(2)}, u32[]{:S(2)}) collective-permute-start(bf16[512,512]{1,0:T(8,128)(2,1)} %param.46), channel_id=1, source_target_pairs={{0,8},{4,12},{8,16},{12,20},{16,24},{20,28},{1,9},{5,13},{9,17},{1... | collective-permute-start | bytes 1572872 | tf_op jit(solution)/shard_map/ppermute | solution.py:19
  166.7 14.6 %collective-permute-start.16 = (bf16[512,512]{1,0:T(8,128)(2,1)}, bf16[512,512]{1,0:T(8,128)(2,1)S(1)}, u32[]{:S(2)}, u32[]{:S(2)}) collective-permute-start(bf16[512,512]{1,0:T(8,128)(2,1)} %param.46), channel_id=1, source_target_pairs={{0,4},{4,8},{8,12},{12,16},{16,20},{20,24},{24,28},{1,5},{5,9},{9,... | collective-permute-start | bytes 1572872 | tf_op jit(solution)/shard_map/ppermute | solution.py:19
  168.7 22.1 %collective-permute-start.12 = (bf16[512,512]{1,0:T(8,128)(2,1)}, bf16[512,512]{1,0:T(8,128)(2,1)S(1)}, u32[]{:S(2)}, u32[]{:S(2)}) collective-permute-start(bf16[512,512]{1,0:T(8,128)(2,1)} %param.46), channel_id=1, source_target_pairs={{4,0},{8,4},{12,8},{16,12},{20,16},{24,20},{28,24},{5,1},{9,5},{13... | collective-permute-start | bytes 1572872 | tf_op jit(solution)/shard_map/ppermute | solution.py:19
  173.0 20.4 %collective-permute-start.21 = (f32[4,512]{1,0:T(4,128)S(1)}, f32[4,512]{1,0:T(4,128)S(1)}, u32[]{:S(2)}, u32[]{:S(2)}) collective-permute-start(f32[4,512]{1,0:T(4,128)S(1)} %log_add_fusion), channel_id=1, source_target_pairs={{0,8},{4,12},{8,16},{12,20},{16,24},{20,28},{1,9},{5,13},{9,17},{1... | collective-permute-start | bytes 24584 | tf_op jit(solution)/shard_map/ppermute | solution.py:19
  175.8 19.5 %collective-permute-start.17 = (f32[4,512]{1,0:T(4,128)S(1)}, f32[4,512]{1,0:T(4,128)S(1)}, u32[]{:S(2)}, u32[]{:S(2)}) collective-permute-start(f32[4,512]{1,0:T(4,128)S(1)} %log_add_fusion), channel_id=1, source_target_pairs={{0,4},{4,8},{8,12},{12,16},{16,20},{20,24},{24,28},{1,5},{5,9},{9,... | collective-permute-start | bytes 24584 | tf_op jit(solution)/shard_map/ppermute | solution.py:19
  179.4 17.9 %collective-permute-start.13 = (f32[4,512]{1,0:T(4,128)S(1)}, f32[4,512]{1,0:T(4,128)S(1)}, u32[]{:S(2)}, u32[]{:S(2)}) collective-permute-start(f32[4,512]{1,0:T(4,128)S(1)} %log_add_fusion), channel_id=1, source_target_pairs={{4,0},{8,4},{12,8},{16,12},{20,16},{24,20},{28,24},{5,1},{9,5},{13... | collective-permute-start | bytes 24584 | tf_op jit(solution)/shard_map/ppermute | solution.py:19
  181.4 88.5 %collective-permute-start.22 = (bf16[512,512]{0,1:T(8,128)(2,1)}, bf16[512,512]{0,1:T(8,128)(2,1)}, u32[]{:S(2)}, u32[]{:S(2)}) collective-permute-start(bf16[512,512]{0,1:T(8,128)(2,1)} %convolution_convert_fusion), channel_id=1, source_target_pairs={{0,8},{4,12},{8,16},{12,20},{16,24},{20,28},{1,9},{5,13},{9,17},{1... | collective-permute-start | bytes 1572872 | tf_op jit(solution)/shard_map/ppermute | solution.py:19
  190.8 81.2 %collective-permute-start.18 = (bf16[512,512]{0,1:T(8,128)(2,1)}, bf16[512,512]{0,1:T(8,128)(2,1)}, u32[]{:S(2)}, u32[]{:S(2)}) collective-permute-start(bf16[512,512]{0,1:T(8,128)(2,1)} %convolution_convert_fusion), channel_id=1, source_target_pairs={{0,4},{4,8},{8,12},{12,16},{16,20},{20,24},{24,28},{1,5},{5,9},{9,... | collective-permute-start | bytes 1572872 | tf_op jit(solution)/shard_map/ppermute | solution.py:19
  203.5 102.6 %collective-permute-start.8 = (bf16[512,512]{1,0:T(8,128)(2,1)}, bf16[512,512]{1,0:T(8,128)(2,1)}, u32[]{:S(2)}, u32[]{:S(2)}) collective-permute-start(bf16[512,512]{1,0:T(8,128)(2,1)} %param.46), channel_id=1, source_target_pairs={{8,0},{12,4},{16,8},{20,12},{24,16},{28,20},{9,1},{13,5},{17,9},{2... | collective-permute-start | bytes 1572872 | tf_op jit(solution)/shard_map/ppermute | solution.py:19
  205.4 100.5 %collective-permute-start.14 = (bf16[512,512]{0,1:T(8,128)(2,1)}, bf16[512,512]{0,1:T(8,128)(2,1)}, u32[]{:S(2)}, u32[]{:S(2)}) collective-permute-start(bf16[512,512]{0,1:T(8,128)(2,1)} %convolution_convert_fusion), channel_id=1, source_target_pairs={{4,0},{8,4},{12,8},{16,12},{20,16},{24,20},{28,24},{5,1},{9,5},{13... | collective-permute-start | bytes 1572872 | tf_op jit(solution)/shard_map/ppermute | solution.py:19
  207.4 98.7 %collective-permute-start.10 = (bf16[512,512]{0,1:T(8,128)(2,1)}, bf16[512,512]{0,1:T(8,128)(2,1)}, u32[]{:S(2)}, u32[]{:S(2)}) collective-permute-start(bf16[512,512]{0,1:T(8,128)(2,1)} %convolution_convert_fusion), channel_id=1, source_target_pairs={{8,0},{12,4},{16,8},{20,12},{24,16},{28,20},{9,1},{13,5},{17,9},{2... | collective-permute-start | bytes 1572872 | tf_op jit(solution)/shard_map/ppermute | solution.py:19
  270.0 36.2 %collective-permute-start.9 = (f32[4,512]{1,0:T(4,128)S(1)}, f32[4,512]{1,0:T(4,128)S(1)}, u32[]{:S(2)}, u32[]{:S(2)}) collective-permute-start(f32[4,512]{1,0:T(4,128)S(1)} %log_add_fusion), channel_id=1, source_target_pairs={{8,0},{12,4},{16,8},{20,12},{24,16},{28,20},{9,1},{13,5},{17,9},{2... | collective-permute-start | bytes 24584 | tf_op jit(solution)/shard_map/ppermute | solution.py:19
  272.0 34.1 %collective-permute-start.11 = (f32[4,512]{1,0:T(4,128)S(1)}, f32[4,512]{1,0:T(4,128)S(1)}, u32[]{:S(2)}, u32[]{:S(2)}) collective-permute-start(f32[4,512]{1,0:T(4,128)S(1)} %bitcast.230), channel_id=1, source_target_pairs={{8,0},{12,4},{16,8},{20,12},{24,16},{28,20},{9,1},{13,5},{17,9},{2... | collective-permute-start | bytes 24584 | tf_op jit(solution)/shard_map/ppermute | solution.py:19
  (28 other events, 362.0 us)
Sparse Core Ops, SparseCore 0:
  10.2 47.1 all-gather.1
  156.2 78.4 reduce-scatter.2
  239.0 51.8 reduce-scatter.4
where the time goes:
time: 343 us; the launch traced here: 338 us
  matrix products  125 us (36%)
  local copies, waits for them, and re-layouts  88.2 us (26%)
  starting transfers between devices  69.6 us (20%)
  other arithmetic  31.3 us (9%)
  between operations  20.4 us (6%)
    ppermute x24, starting transfers between devices, passed_along(): lax.ppermute(value, axis, [(source, source + steps) for source in range(l...  69.5 us
    another operation x12, local copies, waits for them, and re-layouts  53.1 us
    dot_general x8, matrix products, masked_logits(): jnp.einsum('qhd,khd->hqk', query_part, key_part, preferred_element_type=j...  33 us
    cond x5, matrix products, piece_output(): return lax.cond(jnp.any(listed), compute, skipped, 0)  21.5 us
    dot_general x5, matrix products, compute(): jnp.einsum('hqk,khd->qhd', d_logits, key_part, preferred_element_type=jnp...  19.6 us
    dot_general x4, matrix products, compute(): jnp.einsum('hqk,qhd->khd', d_logits, query_part, preferred_element_type=j...  19 us
    dot_general x4, matrix products, compute(): jnp.einsum('hqk,qhd->khd', weights.astype(jnp.bfloat16), grad_part, prefe...  15.8 us
    unnamed x44, local copies, waits for them, and re-layouts  10.9 us
  transfers between devices with their start and end apart: 27, of which 1 were waited for; matrix products, arithmetic and copies ran while one was open for 66% of the time, Pallas kernels for 0%

commit v1 on v0

--- a/solution.py
+++ b/solution.py
@@ -3,6 +3,8 @@
 import jax
 import jax.numpy as jnp
 from jax import lax
+from jax.experimental import pallas as pl
+from jax.experimental.pallas import tpu as pltpu
 from jax.sharding import PartitionSpec as P
 
 HD = 128
@@ -11,6 +13,11 @@
 
 
 FLOOR_LOGIT = -1e30
+SCALE = 1.0 / math.sqrt(HD)
+LOG2_SCALE = SCALE * math.log2(math.e)
+NT = (((1,), (1,)), ((), ()))
+TN = (((0,), (0,)), ((), ()))
+VMEM_LIMIT = 48 * 1024 * 1024
 
 
 def passed_along(value, axis, steps):
@@ -255,6 +262,196 @@
     return (attended, query_grad, key_grad, value_grad, weight_grad)
 
 
+def block_slot(block, parity):
+    return (((block // 2) + parity) % 2) * 8 + (block // 4) * 2 + block % 2
+
+
+def forward_kernel(pattern, counts, parity_ref, q_ref, k_ref, v_ref, out_ref, total_ref, scores):
+    parity = parity_ref[0]
+
+    def query_block(index, carry):
+        block = 4 * (index // 2) + 2 * parity + index % 2
+        entries = counts[block]
+        query = q_ref[index]
+
+        def score(entry, highest):
+            slot = block_slot(pattern[block, entry], parity)
+            logits = (
+                lax.dot_general(k_ref[slot], query, NT, preferred_element_type=jnp.float32)
+                * LOG2_SCALE
+            )
+            scores[entry] = logits
+            return jnp.maximum(highest, jnp.max(logits, axis=0, keepdims=True))
+
+        highest = lax.fori_loop(0, entries, score, jnp.full((1, BLK), FLOOR_LOGIT, jnp.float32))
+
+        def blend(entry, state):
+            total, mixed = state
+            slot = block_slot(pattern[block, entry], parity)
+            weights = jnp.exp2(scores[entry] - highest)
+            total = total + jnp.sum(weights, axis=0, keepdims=True)
+            mixed = mixed + lax.dot_general(
+                v_ref[slot], weights.astype(jnp.bfloat16), TN, preferred_element_type=jnp.float32
+            )
+            return total, mixed
+
+        total, mixed = lax.fori_loop(
+            0,
+            entries,
+            blend,
+            (jnp.zeros((1, BLK), jnp.float32), jnp.zeros((HD, BLK), jnp.float32)),
+        )
+        out_ref[index] = jnp.transpose(mixed / total).astype(jnp.bfloat16)
+        total_ref[index] = highest + jnp.log2(total)
+        return carry
+
+    lax.fori_loop(0, q_ref.shape[0], query_block, 0)
+
+
+def backward_kernel(
+    pattern,
+    counts,
+    parity_ref,
+    q_ref,
+    k_ref,
+    v_ref,
+    out_ref,
+    total_ref,
+    grad_ref,
+    dq_ref,
+    dk_ref,
+    dv_ref,
+    dk_far_ref,
+    dv_far_ref,
+    dk_acc,
+    dv_acc,
+):
+    parity = parity_ref[0]
+    dk_acc[...] = jnp.zeros_like(dk_acc)
+    dv_acc[...] = jnp.zeros_like(dv_acc)
+
+    def query_block(index, carry):
+        block = 4 * (index // 2) + 2 * parity + index % 2
+        query = q_ref[index]
+        grad = grad_ref[index]
+        log_total = total_ref[index]
+        products = grad.astype(jnp.float32) * out_ref[index].astype(jnp.float32)
+        row_dots = jnp.sum(jnp.transpose(products), axis=0, keepdims=True)
+
+        def pair(entry, dq):
+            slot = block_slot(pattern[block, entry], parity)
+            key = k_ref[slot]
+            logits = (
+                lax.dot_general(key, query, NT, preferred_element_type=jnp.float32) * LOG2_SCALE
+            )
+            weights = jnp.exp2(logits - log_total)
+            d_probs = lax.dot_general(v_ref[slot], grad, NT, preferred_element_type=jnp.float32)
+            d_logits = (weights * (d_probs - row_dots)).astype(jnp.bfloat16)
+            dv_acc[slot] += jnp.dot(
+                weights.astype(jnp.bfloat16), grad, preferred_element_type=jnp.float32
+            )
+            dk_acc[slot] += jnp.dot(d_logits, query, preferred_element_type=jnp.float32)
+            return dq + lax.dot_general(key, d_logits, TN, preferred_element_type=jnp.float32)
+
+        dq = lax.fori_loop(0, counts[block], pair, jnp.zeros((HD, BLK), jnp.float32))
+        dq_ref[index] = jnp.transpose(dq * SCALE).astype(jnp.bfloat16)
+        return carry
+
+    lax.fori_loop(0, q_ref.shape[0], query_block, 0)
+    half = dk_acc.shape[0] // 2
+    dk_ref[...] = dk_acc[:half] * SCALE
+    dv_ref[...] = dv_acc[:half]
+    dk_far_ref[...] = (dk_acc[half:] * SCALE).astype(jnp.bfloat16)
+    dv_far_ref[...] = dv_acc[half:].astype(jnp.bfloat16)
+
+
+SMEM_SPEC = pl.BlockSpec(memory_space=pltpu.SMEM)
+VMEM_SPEC = pl.BlockSpec(memory_space=pltpu.VMEM)
+
+
+def local_by_heads(
+    query_heads,
+    key_heads,
+    value_heads,
+    out_weight,
+    cotangent,
+    loss_mask,
+    block_pattern,
+    block_counts,
+):
+    tok_rows, local_cols = query_heads.shape
+    head_count = local_cols // HD
+    seq_devices = lax.axis_size("seq")
+    own_blocks = head_count * tok_rows // BLK
+    groups = [list(range(core, seq_devices, 2)) for core in range(2)]
+    partner = [(source, source ^ 1) for source in range(seq_devices)]
+
+    def exchanged(value):
+        return lax.all_to_all(value, "seq", 0, 0, axis_index_groups=groups, tiled=True)
+
+    def by_head(value):
+        return jnp.transpose(value.reshape(tok_rows, head_count, HD), (1, 0, 2))
+
+    def by_token(value):
+        return jnp.transpose(value, (1, 0, 2)).reshape(tok_rows, local_cols)
+
+    parity = (lax.axis_index("seq") % 2).astype(jnp.int32).reshape(1)
+    masked = jnp.where(loss_mask[:, None] == 1, cotangent, jnp.zeros_like(cotangent))
+    full_grad = lax.all_gather(masked, "tp", axis=1, tiled=True)
+
+    keys_values = exchanged(jnp.stack([by_head(key_heads), by_head(value_heads)], axis=1))
+    far = lax.ppermute(keys_values, "seq", partner)
+    queries = exchanged(by_head(query_heads)).reshape(own_blocks, BLK, HD)
+    keys = jnp.concatenate([keys_values[:, 0], far[:, 0]], 0).reshape(2 * own_blocks, BLK, HD)
+    values = jnp.concatenate([keys_values[:, 1], far[:, 1]], 0).reshape(2 * own_blocks, BLK, HD)
+
+    blocks_bf16 = jax.ShapeDtypeStruct((own_blocks, BLK, HD), jnp.bfloat16)
+    blocks_f32 = jax.ShapeDtypeStruct((own_blocks, BLK, HD), jnp.float32)
+    heads_blocks, log_total = pl.pallas_call(
+        forward_kernel,
+        out_shape=(blocks_bf16, jax.ShapeDtypeStruct((own_blocks, 1, BLK), jnp.float32)),
+        in_specs=[SMEM_SPEC] * 3 + [VMEM_SPEC] * 3,
+        out_specs=(VMEM_SPEC,) * 2,
+        scratch_shapes=[pltpu.VMEM((block_pattern.shape[1], BLK, BLK), jnp.float32)],
+        compiler_params=pltpu.CompilerParams(vmem_limit_bytes=VMEM_LIMIT),
+        name="attention_forward",
+    )(block_pattern, block_counts, parity, queries, keys, values)
+    heads_out = by_token(exchanged(heads_blocks.reshape(head_count, tok_rows, HD)))
+
+    d_heads = jnp.einsum(
+        "td,cd->tc", full_grad, out_weight, preferred_element_type=jnp.float32
+    ).astype(jnp.bfloat16)
+    grads = exchanged(by_head(d_heads)).reshape(own_blocks, BLK, HD)
+
+    partial_out = jnp.dot(heads_out, out_weight, preferred_element_type=jnp.float32)
+    attended = lax.psum_scatter(
+        partial_out.astype(jnp.bfloat16), "tp", scatter_dimension=1, tiled=True
+    )
+    weight_part = jnp.einsum("tc,td->cd", heads_out, full_grad, preferred_element_type=jnp.float32)
+    weight_grad = lax.psum_scatter(
+        weight_part.astype(jnp.bfloat16), "seq", scatter_dimension=1, tiled=True
+    ).astype(jnp.float32)
+
+    dq, dk, dv, dk_far, dv_far = pl.pallas_call(
+        backward_kernel,
+        out_shape=(blocks_bf16, blocks_f32, blocks_f32, blocks_bf16, blocks_bf16),
+        in_specs=[SMEM_SPEC] * 3 + [VMEM_SPEC] * 6,
+        out_specs=(VMEM_SPEC,) * 5,
+        scratch_shapes=[pltpu.VMEM((2 * own_blocks, BLK, HD), jnp.float32)] * 2,
+        compiler_params=pltpu.CompilerParams(vmem_limit_bytes=VMEM_LIMIT),
+        name="attention_backward",
+    )(block_pattern, block_counts, parity, queries, keys, values, heads_blocks, log_total, grads)
+    dk_near, dv_near = lax.ppermute((dk_far, dv_far), "seq", partner)
+    dk = (dk + dk_near.astype(jnp.float32)).astype(jnp.bfloat16)
+    dv = (dv + dv_near.astype(jnp.float32)).astype(jnp.bfloat16)
+    by_source = (head_count, tok_rows, HD)
+    returned = exchanged(
+        jnp.stack([dq.reshape(by_source), dk.reshape(by_source), dv.reshape(by_source)], axis=1)
+    )
+    query_grad, key_grad, value_grad = (by_token(returned[:, part]) for part in range(3))
+    return (attended, query_grad, key_grad, value_grad, weight_grad)
+
+
 def solution(mesh):
     in_specs = (
         P("seq", "tp"),
@@ -267,4 +464,19 @@
         P(),
     )
     out_specs = (P("seq", "tp"), P("seq", "tp"), P("seq", "tp"), P("seq", "tp"), P("tp", "seq"))
-    return jax.shard_map(local, mesh=mesh, in_specs=in_specs, out_specs=out_specs, check_vma=False)
+
+    def run(query_heads, *others):
+        shard = (
+            query_heads.shape[0] // mesh.shape["seq"],
+            query_heads.shape[1] // mesh.shape["tp"],
+        )
+        one_head_a_chip = shard[0] == 2 * BLK and mesh.shape["seq"] == 2 * (shard[1] // HD)
+        return jax.shard_map(
+            local_by_heads if one_head_a_chip else local,
+            mesh=mesh,
+            in_specs=in_specs,
+            out_specs=out_specs,
+            check_vma=False,
+        )(query_heads, *others)
+
+    return run

time: 343 us -> 179 us (0.52)
  the two profiles are of different devices: /device:TPU:2 before, /device:TPU:0 now
where the time goes in v1:
time: 179 us; the launch traced here: 177 us
  blocking collectives  63.1 us (35%)
  waiting for transfers between devices  29.1 us (16%)
  Pallas kernels  27.3 us (15%)
  local copies, waits for them, and re-layouts  20.9 us (12%)
  between operations  13.9 us (8%)
  matrix products  10.6 us (6%)
  other arithmetic  7.45 us (4%)
  starting transfers between devices  4.82 us (3%)
    all_to_all x4, blocking collectives, exchanged(): lax.all_to_all(value, 'seq', 0, 0, axis_index_groups=groups, tiled=True)  63.1 us
    reduce_scatter x1, waiting for transfers between devices, local_by_heads(): lax.psum_scatter(partial_out.astype(jnp.bfloat16), 'tp', scatter_dimensio...  20.6 us
    pallas_call x1, Pallas kernels, local_by_heads(): pl.pallas_call(backward_kernel, out_shape=(blocks_bf16, blocks_f32, block...  14.7 us
    pallas_call x1, Pallas kernels, local_by_heads(): pl.pallas_call(forward_kernel, out_shape=(blocks_bf16, jax.ShapeDtypeStru...  12.6 us
    unnamed x28, local copies, waits for them, and re-layouts  11.8 us
    all_to_all x1, waiting for transfers between devices, exchanged(): lax.all_to_all(value, 'seq', 0, 0, axis_index_groups=groups, tiled=True)  6.41 us
    dot_general x1, matrix products, local_by_heads(): jnp.einsum('tc,td->cd', heads_out, full_grad, preferred_element_type=jnp....  4.32 us
    all_to_all x1, starting transfers between devices, exchanged(): lax.all_to_all(value, 'seq', 0, 0, axis_index_groups=groups, tiled=True)  4.13 us
  transfers between devices with their start and end apart: 7, of which 4 were waited for; matrix products, arithmetic and copies ran while one was open for 16% of the time, Pallas kernels for 15%

profile of v1, /device:TPU:0, one launch (start us, length us, event | category | flops | bytes accessed | tf_op | source)
XLA Modules:
  0.0 177.2 jit_solution(6131433769779777768)
XLA Ops:
  8.1 2.0 %broadcast_select_fusion = bf16[512,512]{1,0:T(8,128)(2,1)} fusion(bf16[512,512]{1,0:T(8,128)(2,1)} %param.12, pred[512]{0:T(512)(128)(4,1)S(1)} %broadcast_compare_fusion), kind=kLoop, calls=%fused_computation.14 | loop fusion | flops 262144 | bytes 1049088 | tf_op jit(solution)/shard_map/jit(_where)/select_n | solution.py:399
  10.1 2.0 %copy.37 = bf16[512,512]{0,1:T(8,128)(2,1)} copy(bf16[512,512]{1,0:T(8,128)(2,1)} %param.9) | data formatting | bytes 1048576 | tf_op args[1]
  13.2 1.3 pad_maximum_fusion.1
  14.5 1.3 copy.39
  15.8 19.4 %all_to_all.25 = bf16[4,2,512,128]{3,2,1,0:T(8,128)(2,1)S(1)} all-to-all(bf16[4,2,512,128]{3,2,1,0:T(8,128)(2,1)} %copy.39), channel_id=1, replica_groups={{0,8,16,24},{4,12,20,28},{1,9,17,25},{5,13,21,29},{2,10,18,26},{6,14,22..., dimensions={0} | all-to-all | bytes 2097152 | tf_op jit(solution)/shard_map/all_to_all | solution.py:390
  37.1 4.1 %all-to-all-start = ((bf16[4,512,128]{2,1,0:T(8,128)(2,1)}), bf16[4,512,128]{2,1,0:T(8,128)(2,1)}, u32[]{:S(2)}, u32[]{:S(2)}) async-start(bf16[4,512,128]{2,1,0:T(8,128)(2,1)} %bitcast_bitcast_fusion), calls=%async_computation | async-start | bytes 1048576 | tf_op jit(solution)/shard_map/all_to_all | solution.py:390
  41.4 1.3 slice_bitcast_fusion
  43.9 6.4 %all-to-all-done = bf16[4,512,128]{2,1,0:T(8,128)(2,1)} async-done(((bf16[4,512,128]{2,1,0:T(8,128)(2,1)}), bf16[4,512,128]{2,1,0:T(8,128)(2,1)}, u32[]{:S(2)}, u32[]{:S(2)}) %all-to-all-start) | async-done | bytes 524320 | tf_op jit(solution)/shard_map/all_to_all | solution.py:390
  50.3 1.2 copy-done.2
  51.5 12.6 %attention_forward.1 = (bf16[8,256,128]{2,1,0:T(8,128)(2,1)S(1)}, f32[8,1,256]{2,1,0:T(1,128)S(1)}) custom-call(s32[16,9]{1,0:T(8,128)S(1)} %copy-done.5, s32[16]{0:T(128)S(1)} %copy-done.6, s32[1]{0:T(128)} %bitcast.parity_ref, bf16[8,256,128]{2,1,0:T(8,128)(2,1)} %bitcast.2.q_ref, bf16[16,256,128]{2,1,0:T(8,128)(2,1)S(1)} %bitcast.66, ...), custom_call_target="tpu_custom_call" | custom-call | tf_op jit(solution)/shard_map/attention_forward/pallas_call | solution.py:410
  64.9 2.0 %copy.42 = bf16[4,512,128]{1,2,0:T(8,128)(2,1)} copy(bf16[4,512,128]{2,1,0:T(8,128)(2,1)} %bitcast.70) | data formatting | bytes 1048576 | tf_op jit(solution)/shard_map/reshape | solution.py:419
  67.0 11.3 %all_to_all.26 = bf16[4,512,128]{1,2,0:T(8,128)(2,1)} all-to-all(bf16[4,512,128]{1,2,0:T(8,128)(2,1)} %copy.42), channel_id=1, replica_groups={{0,8,16,24},{4,12,20,28},{1,9,17,25},{5,13,21,29},{2,10,18,26},{6,14,22..., dimensions={0} | all-to-all | bytes 1048576 | tf_op jit(solution)/shard_map/all_to_all | solution.py:390
  78.3 4.3 %convolution_convert_fusion = bf16[512,2048]{1,0:T(8,128)(2,1)} fusion(bf16[512,512]{0,1:T(8,128)(2,1)} %bitcast.81, bf16[512,2048]{1,0:T(8,128)(2,1)} %all-gather.2.cloned.1.call-done), kind=kOutput, calls=%fused_computation | convolution fusion | flops 1074790400 | bytes 4718592 | tf_op jit(solution)/shard_map/tc,td->cd/dot_general | solution.py:430
  83.7 2.6 %convolution_convert_fusion.1 = bf16[512,2048]{1,0:T(8,128)(2,1)} fusion(bf16[512,512]{0,1:T(8,128)(2,1)S(1)} %bitcast.82, bf16[512,2048]{1,0:T(8,128)(2,1)S(1)} %copy-done), kind=kOutput, calls=%fused_computation.1 | convolution fusion | flops 1074790400 | bytes 4718592 | tf_op jit(solution)/shard_map/dot_general | solution.py:426
  86.3 3.7 %convolution_convert_fusion.2 = bf16[512,512]{0,1:T(8,128)(2,1)} fusion(bf16[512,2048]{1,0:T(8,128)(2,1)} %all-gather.2.cloned.1.call-done, bf16[512,2048]{1,0:T(8,128)(2,1)S(1)} %copy-done), kind=kOutput, calls=%fused_computation.3 | convolution fusion | flops 1074003968 | bytes 4718592 | tf_op jit(solution)/shard_map/td,cd->tc/dot_general | solution.py:421
  90.0 1.5 copy.43
  91.5 9.5 %all_to_all.27 = bf16[4,512,128]{2,1,0:T(8,128)(2,1)S(1)} all-to-all(bf16[4,512,128]{2,1,0:T(8,128)(2,1)S(1)} %bitcast.73), channel_id=1, replica_groups={{0,8,16,24},{4,12,20,28},{1,9,17,25},{5,13,21,29},{2,10,18,26},{6,14,22..., dimensions={0} | all-to-all | bytes 1048576 | tf_op jit(solution)/shard_map/all_to_all | solution.py:390
  101.0 14.7 %attention_backward.1 = (bf16[8,256,128]{2,1,0:T(8,128)(2,1)S(1)}, f32[8,256,128]{2,1,0:T(8,128)S(1)}, f32[8,256,128]{2,1,0:T(8,128)S(1)}, bf16[8,256,128]{2,1,0:T(8,128)(2,1)S(1)}, bf16[8,256,128]{2,1,0:T(8,128)(2,1)S(1)}) custom-call(s32[16,9]{1,0:T(8,128)S(1)} %copy-done.5, s32[16]{0:T(128)S(1)} %copy-done.6, s32[1]{0:T(128)} %bitcast.parity_ref, ...), custom_call_target="tpu_custom_call" | custom-call | tf_op jit(solution)/shard_map/attention_backward/pallas_call | solution.py:435
  116.3 1.4 collective-permute-done.1
  118.7 22.8 %all_to_all.28 = bf16[4,3,512,128]{3,2,1,0:T(8,128)(2,1)S(1)} all-to-all(bf16[4,3,512,128]{3,2,1,0:T(8,128)(2,1)S(1)} %pad_maximum_fusion), channel_id=1, replica_groups={{0,8,16,24},{4,12,20,28},{1,9,17,25},{5,13,21,29},{2,10,18,26},{6,14,22..., dimensions={0} | all-to-all | bytes 3145728 | tf_op jit(solution)/shard_map/all_to_all | solution.py:390
  142.6 1.2 copy.55
  144.9 1.3 copy.54
  148.4 1.8 %convert_element_type.31 = f32[512,256]{1,0:T(8,128)} convert(bf16[512,256]{1,0:T(8,128)(2,1)} %reduce-scatter.5.cloned.1.call-done) | non-fusion elementwise | flops 131072 | bytes 786432 | tf_op jit(solution)/shard_map/convert_element_type | solution.py:433
  150.1 20.6 %reduce-scatter.3.cloned.1.call-done = bf16[512,512]{1,0:T(8,128)(2,1)} async-done(((bf16[512,2048]{1,0:T(8,128)(2,1)}), bf16[512,512]{1,0:T(8,128)(2,1)}) %reduce-scatter.3.cloned.1.call-update) | async-done | bytes 524304 | tf_op jit(solution)/shard_map/reduce_scatter | solution.py:427
  (47 shorter events, 12.9 us)
Async XLA Ops:
  7.2 75.5 %copy-start = (bf16[512,2048]{1,0:T(8,128)(2,1)S(1)}, bf16[512,2048]{1,0:T(8,128)(2,1)}, u32[]{:S(2)}) copy-start(bf16[512,2048]{1,0:T(8,128)(2,1)} %param.11) | copy-start | bytes 6291460
  7.2 5.0 %copy-start.7 = (bf16[512,512]{1,0:T(8,128)(2,1)S(1)}, bf16[512,512]{1,0:T(8,128)(2,1)}, u32[]{:S(2)}) copy-start(bf16[512,512]{1,0:T(8,128)(2,1)} %param.10) | copy-start | bytes 1572868
  7.2 71.1 %all-gather.2.cloned.1.call-start = ((), (), s32[]{:S(2)}) async-start(), calls=%async_computation.8 | async-start | bytes 2621440 | tf_op jit(solution)/shard_map/all_gather | solution.py:400
  15.8 20.5 %copy-start.8 = (bf16[512,512]{1,0:T(8,128)(2,1)S(1)}, bf16[512,512]{1,0:T(8,128)(2,1)}, u32[]{:S(2)}) copy-start(bf16[512,512]{1,0:T(8,128)(2,1)} %param.8) | copy-start | bytes 1572868
  36.2 5.2 %collective-permute-start = (bf16[4,2,512,128]{3,2,0,1:T(8,128)(2,1)}, bf16[4,2,512,128]{3,2,0,1:T(8,128)(2,1)}, u32[]{:S(2)}, u32[]{:S(2)}) collective-permute-start(bf16[4,2,512,128]{3,2,0,1:T(8,128)(2,1)} %copy.40), channel_id=1, source_target_pairs={{0,4},{4,0},{8,12},{12,8},{16,20},{20,16},{24,28},{28,24},{1,5},{5... | collective-permute-start | bytes 3145736 | tf_op jit(solution)/shard_map/ppermute | solution.py:403
  37.1 13.2 %all-to-all-start = ((bf16[4,512,128]{2,1,0:T(8,128)(2,1)}), bf16[4,512,128]{2,1,0:T(8,128)(2,1)}, u32[]{:S(2)}, u32[]{:S(2)}) async-start(bf16[4,512,128]{2,1,0:T(8,128)(2,1)} %bitcast_bitcast_fusion), calls=%async_computation | async-start | bytes 1048576 | tf_op jit(solution)/shard_map/all_to_all | solution.py:390
  41.3 107.1 %reduce-scatter.5.cloned.1.call-start = ((), (), s32[]{:S(2)}) async-start(), calls=%async_computation.9 | async-start | bytes 2359296 | tf_op jit(solution)/shard_map/reduce_scatter | solution.py:431
  42.7 7.6 %copy-start.5 = (s32[16,9]{1,0:T(8,128)S(1)}, s32[16,9]{1,0:T(8,128)}, u32[]{:S(2)}) copy-start(s32[16,9]{1,0:T(8,128)} %pattern.3) | copy-start | bytes 1732
  42.7 7.6 %copy-start.6 = (s32[16]{0:T(128)S(1)}, s32[16]{0:T(128)}, u32[]{:S(2)}) copy-start(s32[16]{0:T(128)} %counts.3) | copy-start | bytes 196
  43.9 34.4 %copy-start.1 = (bf16[8,512,128]{2,1,0:T(8,128)(2,1)}, bf16[8,512,128]{2,1,0:T(8,128)(2,1)S(1)}, u32[]{:S(2)}) copy-start(bf16[8,512,128]{2,1,0:T(8,128)(2,1)S(1)} %get-tuple-element.29) | copy-start | bytes 3145732
  50.3 1.2 copy-start.2
  64.1 0.8 copy-start.3
  82.6 1.0 copy-start.9
  82.7 88.0 %reduce-scatter.3.cloned.1.call-start = ((), (), s32[]{:S(2)}) async-start(), calls=%async_computation.7 | async-start | bytes 2621440 | tf_op jit(solution)/shard_map/reduce_scatter | solution.py:427
  90.0 11.0 %copy-start.4 = (bf16[8,256,128]{2,1,0:T(8,128)(2,1)S(1)}, bf16[8,256,128]{2,1,0:T(8,128)(2,1)}, u32[]{:S(2)}) copy-start(bf16[8,256,128]{2,1,0:T(8,128)(2,1)} %copy-done.3) | copy-start | bytes 1572868
  115.7 2.0 %collective-permute-start.1 = (bf16[8,256,128]{2,1,0:T(8,128)(2,1)S(1)}, bf16[8,256,128]{2,1,0:T(8,128)(2,1)S(1)}, u32[]{:S(2)}, u32[]{:S(2)}) collective-permute-start(bf16[8,256,128]{2,1,0:T(8,128)(2,1)S(1)} %get-tuple-element.16), channel_id=1, source_target_pairs={{0,4},{4,0},{8,12},{12,8},{16,20},{20,16},{24,28},{28,24},{1,5},{5... | collective-permute-start | bytes 1572872 | tf_op jit(solution)/shard_map/ppermute | solution.py:444
  115.8 2.6 %collective-permute-start.2 = (bf16[8,256,128]{2,1,0:T(8,128)(2,1)S(1)}, bf16[8,256,128]{2,1,0:T(8,128)(2,1)S(1)}, u32[]{:S(2)}, u32[]{:S(2)}) collective-permute-start(bf16[8,256,128]{2,1,0:T(8,128)(2,1)S(1)} %get-tuple-element.18), channel_id=1, source_target_pairs={{0,4},{4,0},{8,12},{12,8},{16,20},{20,16},{24,28},{28,24},{1,5},{5... | collective-permute-start | bytes 1572872 | tf_op jit(solution)/shard_map/ppermute | solution.py:444
Sparse Core Ops, SparseCore 0:
  10.2 48.6 all-gather.1
  82.8 40.9 reduce-scatter.4
  126.8 43.8 reduce-scatter.2
